TPU v7x, 128 devices: a whole 4x4x4 slice. The times are simulated.
128 devices in a mesh: lon: 32 (over z_hi, x, y), lat: 4 (over z_lo, core).
Axes of the slice: x: 4, y: 4, z: 4 (z_hi: 2, z_lo: 2; z = z_hi * 2 + z_lo), core: 2. Of those that a mesh axis runs over, the one named last changes fastest.
Arguments:
- patch_rows: bfloat16 [262144, 512], P(('lon', 'lat')), may hold values from -400 to 400
- source_embed: bfloat16 [4, 512], replicated, may hold values from -6 to 6
- cell_embed: bfloat16 [512, 128, 512], P('lon', 'lat'), may hold values from -6 to 6
- level_query: bfloat16 [4, 512], replicated, may hold values from -6 to 6
- margin_rows: int32 [128, 3, 3, 128], P(('lon', 'lat')), may hold values from 0 to 2047, as said below
- margin_counts: int32 [128, 3, 3], P(('lon', 'lat')), may hold values from 0 to 128, as said below
- query_weight: bfloat16 [512, 512], replicated, may hold values from -0.25 to 0.25
- key_weight: bfloat16 [512, 512], replicated, may hold values from -0.25 to 0.25
- value_weight: bfloat16 [512, 512], replicated, may hold values from -0.25 to 0.25
- out_weight: bfloat16 [512, 512], replicated, may hold values from -0.25 to 0.25
- conv_weight: bfloat16 [2, 3, 3, 512, 512], replicated, may hold values from -0.09375 to 0.09375
Outputs:
- latent: bfloat16 [512, 128, 4, 512], P('lon', 'lat')
Inputs may be any that keep to these rules, and one draw needn't show every extreme that they name: margin_rows[s, a, b, j] is a local row of device s. `margin_counts`: a list whose source device lies outside the latitude range has count 0; every other list, the owner's own among them, has at least one live row; in every draw some tile owner receives 128 rows from every source device beside it.
All inputs are finite; a program needn't handle non-finite values.
Results may differ from a plain program's by a relative error of at most 0.009.
The roundings to bfloat16 on the way count: a program that leaves them out, or rounds other values in their place, can miss the bound.
Values may be sent and summed in bfloat16 or wider, within the bound.
No kernel may reach another device: no remote copies, remote signals or barrier semaphores. Data moves between devices by JAX's collectives and lax.ppermute only.
A program may use at most 192 MiB of HBM per device.

v0:
```python
import functools
import math

import jax
import jax.numpy as jnp
from jax import lax
from jax.experimental import pallas as pl
from jax.experimental.pallas import tpu as pltpu
from jax.sharding import PartitionSpec as P

D = 512
HEADS = 16
HEAD = 32
CAP = 128
LON = 16
LAT = 32
CELLS = LON * LAT
LEVELS = 4
KEYS = 9 * CAP
SCALE = 1.0 / math.sqrt(HEAD)
LOG2E = 1.4426950408889634
CALM = 90.0
F32 = jnp.float32
BF16 = jnp.bfloat16
MIB = 1024 * 1024
NT = (((1,), (1,)), ((), ()))
TN = (((0,), (0,)), ((), ()))
AXES = ("lon", "lat")


def dot(a, b, dims=(((1,), (0,)), ((), ()))):
    return lax.dot_general(a, b, dims, preferred_element_type=F32)


def iota(shape, dim):
    return lax.broadcasted_iota(jnp.int32, shape, dim)


def gather_kernel(lat_ref, rows_hbm, embed_hbm, index_hbm, east_ref, west_ref, one_ref, two_ref, own_ref,
                  raw, total, column, embed_ref, index_ref, sems):
    copies = [
        pltpu.make_async_copy(rows_hbm.at[pl.ds(s * 512, 512)], raw.at[s], sems.at[s])
        for s in range(4)
    ]
    small = [
        pltpu.make_async_copy(index_hbm, index_ref, sems.at[4]),
        pltpu.make_async_copy(embed_hbm, embed_ref, sems.at[5]),
    ]
    for copy in small + copies:
        copy.start()
    for copy in small:
        copy.wait()
    odd = lax.rem(lat_ref[0], 2)
    for n, a in enumerate((2, 0, 1)):
        for slot in range(3):
            if slot == 2:
                want = index_ref[3 * a + 1]
            else:
                low, high = index_ref[3 * a], index_ref[3 * a + 2]
                even_pick, odd_pick = (high, low) if slot == 0 else (low, high)
                want = jnp.where(odd == 1, odd_pick, even_pick)
            start = (3 * n + slot) * CAP
            column[start : start + CAP, :] = jnp.broadcast_to(want, (CAP, CAP)).T
    total[...] = jnp.zeros_like(total)
    embeds = embed_ref[...].astype(F32)

    def source(s, carry):
        pltpu.make_async_copy(rows_hbm.at[pl.ds(s * 512, 512)], raw.at[s], sems.at[s]).wait()
        embed = jnp.sum(jnp.where(iota((4, D), 0) == s, embeds, 0.0), axis=0, keepdims=True)
        rows = (raw[s].astype(F32) + embed).astype(BF16)
        local = column[...] - s * 512
        lane = iota((9 * CAP, 128), 1)
        picks = jnp.concatenate([(lane + 128 * k == local).astype(F32).astype(BF16) for k in range(4)], axis=1)
        total[...] += dot(picks, rows)
        return carry

    lax.fori_loop(0, 4, source, 0)
    three = 3 * CAP
    east_ref[...] = total[:three].astype(BF16).reshape(3, CAP, D)
    west_ref[...] = total[three : 2 * three].astype(BF16).reshape(3, CAP, D)
    one_ref[...] = total[2 * three : 2 * three + CAP].astype(BF16)
    two_ref[...] = total[2 * three + CAP : 2 * three + 2 * CAP].astype(BF16)
    own_ref[...] = total[2 * three + 2 * CAP :].astype(BF16)


def gather(lat, patch_rows, source_embed, margin_rows):
    vmem = pl.BlockSpec(memory_space=pltpu.VMEM)
    three = jax.ShapeDtypeStruct((3, CAP, D), BF16)
    single = jax.ShapeDtypeStruct((CAP, D), BF16)
    return pl.pallas_call(
        gather_kernel,
        out_shape=(three, three, single, single, single),
        in_specs=[pl.BlockSpec(memory_space=pltpu.SMEM)] + [pl.BlockSpec(memory_space=pltpu.HBM)] * 3,
        out_specs=(vmem,) * 5,
        scratch_shapes=[
            pltpu.VMEM((4, 512, D), BF16), pltpu.VMEM((9 * CAP, D), F32), pltpu.VMEM((9 * CAP, 128), jnp.int32),
            pltpu.VMEM((4, D), BF16),
            pltpu.VMEM((9, 1, CAP), jnp.int32), pltpu.SemaphoreType.DMA((6,)),
        ],
        compiler_params=pltpu.CompilerParams(vmem_limit_bytes=59 * MIB),
        name="gather_rows",
    )(lat, patch_rows, source_embed, margin_rows.reshape(9, 1, CAP))


def gain_of(lat, shape, dim):
    row = (lat * LAT + iota(shape, dim)).astype(F32)
    phi = (row + 0.5) / 128 * jnp.pi - jnp.pi / 2
    return 0.5 + jnp.cos(phi)


def normal(x, gain):
    spread = jnp.sqrt(jnp.mean(x * x, axis=-1, keepdims=True) + 1e-06)
    return x / spread * gain


def edge_pick():
    row, col = iota((2 * LON, CELLS), 0), iota((2 * LON, CELLS), 1)
    return (col == row % LON * LAT + row // LON * (LAT - 1)).astype(F32).astype(BF16)


def pair_rows(lat, lev, north, south, gain, one_ref, two_ref):
    north = normal(north, gain[0:1, :])
    south = normal(south, gain[LAT - 1 :, :])
    odd = lax.rem(lat, 2) == 1
    one_ref[lev] = jnp.where(odd, north, south).astype(BF16)
    two_ref[lev] = jnp.where(odd, south, north).astype(BF16)


def head_norms(values):
    heads = (iota((D, 128), 0) // HEAD == iota((D, 128), 1)).astype(F32).astype(BF16)
    return jnp.max(dot((values * values).astype(BF16), heads), axis=0, keepdims=True)


def project_keys(rows_list, counts, wk, wv, k_s, v_s, live):
    for n, (rows, count) in enumerate(zip(rows_list, counts)):
        live[n * CAP : (n + 1) * CAP, :] = (iota((CAP, 128), 0) < count).astype(F32)
    rows = jnp.concatenate(rows_list, axis=0)
    keys = dot(rows, wk).astype(BF16)
    k_s[...] = keys
    v_s[...] = dot(rows, wv).astype(BF16)
    return head_norms(keys.astype(F32))


def head_group(hg, k_s, v_s, live, q_s, level_block):
    lanes = pl.ds(pl.multiple_of(hg * 128, 128), 128)
    kg, vg, qg = k_s[:, lanes], v_s[:, lanes], q_s[:, lanes]
    group_lane = iota((1, 128), 1) // HEAD
    col, row = iota((128, 512), 1), iota((128, 512), 0)
    copies = ((row // HEAD == col // 128) & (row % HEAD == col % HEAD)).astype(F32).astype(BF16)
    level_exp = jnp.exp2(dot(kg, level_block))
    vals = dot(vg, copies)
    alive = live[...]
    out = []
    for i in range(4):
        span = slice(i * 128, (i + 1) * 128)
        part = level_exp[:, span] * alive
        weighted = jnp.concatenate([part * vals[:, span], part], axis=1).astype(BF16)
        km = jnp.where(group_lane == i, kg, jnp.zeros_like(kg))
        probs = jnp.exp2(dot(qg, km, NT)).astype(BF16)
        out.append(dot(probs, weighted))
    return out


def list_counts(lat_ref, count_ref, part):
    odd = lax.rem(lat_ref[0], 2)
    first, second = 2 - 2 * odd, 2 * odd
    where = (
        ((1, 1), (1, first), (1, second)),
        ((0, 1), (2, 1)),
        ((0, first), (2, first), (0, second), (2, second)),
    )[part]
    return [count_ref[c, 0, r] for c, r in where]


def first_kernel(lat_ref, count_ref, own, one, two, cell_ref, level_ref, wq_ref, wk_ref, wv_ref,
                 sum_ref, q_ref, block_ref, norm_ref, k_s, v_s, live):

    counts = list_counts(lat_ref, count_ref, 0)
    norm_ref[2:3, :] = project_keys([own[...], one[...], two[...]], counts, wk_ref[...], wv_ref[...], k_s, v_s, live)
    level = jnp.concatenate([level_ref[...], level_ref[...]], axis=0)
    qc = dot(cell_ref[...], wq_ref[...]) * (SCALE * LOG2E)
    ql = dot(level, wq_ref[...]) * (SCALE * LOG2E)
    q_ref[...] = qc.astype(BF16)
    norm_ref[0:1, :] = head_norms(qc)
    norm_ref[1:2, :] = head_norms(ql)
    col, row = iota((128, 512), 1), iota((128, 512), 0)
    wide = iota((8, 512), 1)
    pick = (wide // HEAD % 4 - wide // 128 + 4) % 4
    choose = ((iota((8, 512), 0) == pick) & (iota((8, 512), 0) < 4)).astype(F32).astype(BF16)
    for g in range(4):
        spread = dot(ql[:, g * 128 : (g + 1) * 128].astype(BF16), choose, TN)
        block_ref[g] = jnp.where(row // HEAD == col // 128, spread, 0.0).astype(BF16)

    def group(hg, carry):
        for i, both in enumerate(head_group(hg, k_s, v_s, live, q_ref, block_ref[hg])):
            sum_ref[hg, i] = both
        return carry

    lax.fori_loop(0, 4, group, 0)


def second_kernel(lat_ref, count_ref, west, east, sum_in, q_ref, block_ref, wk_ref, wv_ref,
                  sum_ref, norm_ref, k_s, v_s, live):

    counts = list_counts(lat_ref, count_ref, 1)
    norm_ref[0:1, :] = project_keys([west[2], east[2]], counts, wk_ref[...], wv_ref[...], k_s, v_s, live)

    def group(hg, carry):
        for i, both in enumerate(head_group(hg, k_s, v_s, live, q_ref, block_ref[hg])):
            sum_ref[hg, i] = sum_in[hg, i] + both
        return carry

    lax.fori_loop(0, 4, group, 0)


def plain_attention(lists, counts, cell_ref, level_ref, wq_ref, wk_ref, wv_ref, k_all, v_all, q_s, live_row, att):
    for n, (rows, count) in enumerate(zip(lists, counts)):
        span = slice(n * CAP, (n + 1) * CAP)
        k_all[span, :] = rows
        live_row[:, span] = (iota((8, CAP), 1) < count).astype(F32)

    def project(n, carry):
        span = pl.ds(pl.multiple_of(n * CAP, CAP), CAP)
        rows = k_all[span, :]
        v_all[span, :] = dot(rows, wv_ref[...]).astype(BF16)
        k_all[span, :] = dot(rows, wk_ref[...]).astype(BF16)
        return carry

    lax.fori_loop(0, 9, project, 0)
    group_lane = iota((1, 128), 1) // HEAD
    block = 128

    def step(n, carry):
        lev, part = n // 4, n % 4
        cells = pl.ds(pl.multiple_of(part * block, block), block)
        four = level_ref[...].astype(F32)
        mine = jnp.sum(jnp.where(iota((LEVELS, D), 0) == lev, four, 0.0), axis=0, keepdims=True)
        latent = (cell_ref[cells, :].astype(F32) + mine).astype(BF16)
        q_s[...] = dot(latent, wq_ref[...]).astype(BF16)

        def group(hg, carry):
            lanes = pl.ds(pl.multiple_of(hg * 128, 128), 128)
            kg, vg, qg = k_all[:, lanes], v_all[:, lanes], q_s[:, lanes]

            def head(i, total):
                mine = group_lane == i
                scores = dot(qg, jnp.where(mine, kg, jnp.zeros_like(kg)), NT) * SCALE
                scores = jnp.where(live_row[0:1, :] > 0.5, scores, -1e30)
                top = jnp.max(scores, axis=1, keepdims=True)
                weights = jnp.exp(scores - top)
                probs = (weights / jnp.sum(weights, axis=1, keepdims=True)).astype(BF16)
                return total + dot(probs, jnp.where(mine, vg, jnp.zeros_like(vg)))

            total = lax.fori_loop(0, 4, head, jnp.zeros((block, 128), F32))
            att[lev, cells, lanes] = total.astype(BF16)
            return carry

        return lax.fori_loop(0, 4, group, carry)

    lax.fori_loop(0, 4 * LEVELS, step, 0)


def third_kernel(lat_ref, count_ref, own, one_own, two_own, west, east, one, two, sum_in, q_ref, block_ref,
                 norm_a, norm_b, cell_ref, level_ref, wq_ref, wk_ref, wv_ref, wo_ref,
                 x_ref, west_ref, east_ref, one_ref, two_ref,
                 k_s, v_s, live, att, k_all, v_all, q_s, live_row):

    counts = list_counts(lat_ref, count_ref, 2)
    keys = project_keys([one[0], one[1], two[0], two[1]], counts, wk_ref[...], wv_ref[...], k_s, v_s, live)
    keys = jnp.maximum(jnp.maximum(keys, norm_a[2:3, :]), norm_b[0:1, :])
    bound = jnp.sqrt(norm_a[0:1, :] * keys) + jnp.sqrt(norm_a[1:2, :] * keys)
    calm = jnp.max(bound) < CALM

    @pl.when(calm)
    def _():
        group_lane = iota((1, 128), 1) // HEAD

        def group(hg, carry):
            lanes = pl.ds(pl.multiple_of(hg * 128, 128), 128)
            kept = []
            for i, both in enumerate(head_group(hg, k_s, v_s, live, q_ref, block_ref[hg])):
                both = sum_in[hg, i] + both
                kept.append(both[:, :128] / both[:, 128:])
            for lev in range(LEVELS):
                z = kept[0]
                for i in range(4):
                    z = jnp.where(group_lane == (i + lev) % 4, kept[i], z)
                if lev:
                    z = pltpu.roll(z, 128 - HEAD * lev, axis=1)
                att[lev, :, lanes] = z.astype(BF16)
            return carry

        lax.fori_loop(0, 4, group, 0)

    @pl.when(jnp.logical_not(calm))
    def _():
        lists = [own[...], one_own[...], two_own[...], west[2], east[2], one[0], one[1], two[0], two[1]]
        counts = sum((list_counts(lat_ref, count_ref, part) for part in range(3)), [])
        plain_attention(lists, counts, cell_ref, level_ref, wq_ref, wk_ref, wv_ref, k_all, v_all, q_s, live_row, att)

    gain = gain_of(lat_ref[0], (LAT, D), 0)
    pick = edge_pick()
    for lev in range(LEVELS):
        latent = (cell_ref[...].astype(F32) + level_ref[lev : lev + 1, :].astype(F32)).astype(BF16)
        x = (latent.astype(F32) + dot(att[lev], wo_ref[...])).astype(BF16)
        x_ref[lev] = x
        edge_rows = dot(pick, x)
        west_ref[lev] = normal(x[:LAT, :].astype(F32), gain).astype(BF16)
        east_ref[lev] = normal(x[CELLS - LAT :, :].astype(F32), gain).astype(BF16)
        pair_rows(lat_ref[0], lev, edge_rows[:LON], edge_rows[LON:], gain, one_ref, two_ref)


def attend_call(kernel, operands, outs, scratch, flops, alias, name):
    return call(kernel, operands, [(out, "v") for out in outs], scratch, flops, name, alias)


def part_scratch(keys):
    return [pltpu.VMEM((keys, D), BF16), pltpu.VMEM((keys, D), BF16), pltpu.VMEM((keys, 128), F32)]


def attention(lat, counts, own, one_own, two_own, exchange, cells, level_query, wq, wk, wv, wo):
    shape = jax.ShapeDtypeStruct
    sums = shape((4, 4, CELLS, 256), F32)
    norms = shape((8, 128), F32)
    each = 2 * CELLS * D * 8 * 2
    total, q, block, norm_a = attend_call(
        first_kernel,
        [(lat, "s"), (counts, "s"), (own, "v"), (one_own, "v"), (two_own, "v"), (cells, "v"), (level_query, "v"),
         (wq, "v"), (wk, "v"), (wv, "v")],
        [sums, shape((CELLS, D), BF16), shape((4, 128, 512), BF16), norms],
        part_scratch(3 * CAP), each * 3 * CAP, {}, "attend_first",
    )
    west, east, one, two = exchange(norm_a)
    total, norm_b = attend_call(
        second_kernel,
        [(lat, "s"), (counts, "s"), (west, "v"), (east, "v"), (total, "v"), (q, "v"), (block, "v"), (wk, "v"), (wv, "v")],
        [sums, norms],
        part_scratch(2 * CAP), each * 2 * CAP, {4: 0}, "attend_second",
    )
    return attend_call(
        third_kernel,
        [(lat, "s"), (counts, "s"), (own, "v"), (one_own, "v"), (two_own, "v"), (west, "v"), (east, "v"), (one, "v"),
         (two, "v"), (total, "v"), (q, "v"), (block, "v"), (norm_a, "v"), (norm_b, "v"), (cells, "v"),
         (level_query, "v"), (wq, "v"), (wk, "v"), (wv, "v"), (wo, "v")],
        [shape((LEVELS, rows, D), BF16) for rows in (CELLS, LAT, LAT, LON, LON)],
        part_scratch(4 * CAP)
        + [pltpu.VMEM((LEVELS, CELLS, D), BF16), pltpu.VMEM((KEYS, D), BF16),
           pltpu.VMEM((KEYS, D), BF16), pltpu.VMEM((128, D), BF16), pltpu.VMEM((8, KEYS), F32)],
        each * 4 * CAP, {}, "attend_third",
    )


def gelu(total):
    return 0.5 * total * (1.0 + lax.erf(total * (2.0 ** -0.5)))


def read_x(x_refs, lev, low, high):
    if len(x_refs) == 1:
        return x_refs[0][lev, low * LAT : high * LAT, :].astype(F32)
    inner, inner_b, outer, rim = x_refs
    parts = []
    for lon in range(low, high):
        if 4 <= lon < 8:
            part = inner[lev, (lon - 4) * LAT : (lon - 3) * LAT, :]
        elif 8 <= lon < 12:
            part = inner_b[lev, (lon - 8) * LAT : (lon - 7) * LAT, :]
        else:
            place = lon if lon < 4 else lon - 8
            part = outer[lev, place * LAT : (place + 1) * LAT, :]
        parts.append(part.astype(F32))
    rows = jnp.concatenate(parts, axis=0).reshape(high - low, LAT, D)
    edge = rim[lev].astype(F32)
    place = iota((high - low, LAT, D), 1)
    rows = jnp.where(place == 0, edge[low:high][:, None, :], rows)
    rows = jnp.where(place == LAT - 1, edge[LON + low : LON + high][:, None, :], rows)
    return rows.reshape((high - low) * LAT, D)


def interleave(stage, start, levels):
    row, col = iota((256, 256), 0), iota((256, 256), 1)
    order = (col == row % LEVELS * 64 + row // LEVELS).astype(F32).astype(BF16)
    for half in range(2):
        rows = jnp.concatenate([y[half * 64 : half * 64 + 64] for y in levels], axis=0)
        stage[start + half * 64 : start + half * 64 + 64] = dot(order, rows).astype(BF16).reshape(64, LEVELS, D)


def three_shifts(near, wide):
    count = wide.shape[0]
    row = iota((count, D), 0) % LAT
    near[:, 0:D] = jnp.where(row == 0, 0.0, pltpu.roll(wide, 1, axis=0)).astype(BF16)
    near[:, D : 2 * D] = wide.astype(BF16)
    near[:, 2 * D :] = jnp.where(row == LAT - 1, 0.0, pltpu.roll(wide, count - 1, axis=0)).astype(BF16)


def finish(layer, total, x_refs, start, out_ref, place, stage):
    moved = gelu(total)
    levels = []
    for lev in range(LEVELS):
        levels.append((read_x(x_refs, lev, start, start + 4) + moved[lev * 128 : (lev + 1) * 128]).astype(BF16))
        if not layer:
            out_ref[lev, place : place + 128, :] = levels[lev]
    if layer:
        interleave(stage, place, levels)


def inner_kernel(layer, parts, half, lat_ref, *refs):
    x_refs, refs = refs[:parts], refs[parts:]
    w_ref, refs = refs[0], refs[1:]
    if half == 0:
        tied, out_ref, passed = refs[:3]
        refs = refs[3:]
        passed[...] = tied[...]
    elif layer:
        _, out_ref = refs[:2]
        refs = refs[2:]
    else:
        out_ref, refs = refs[0], refs[1:]
    near, stage = refs[0], refs[1:]
    start = 4 + 4 * half
    gain = gain_of(lat_ref[0], (LAT, D), 0)
    gains = jnp.concatenate([gain] * 6, axis=0)
    for lev in range(LEVELS):
        wide = normal(read_x(x_refs, lev, start - 1, start + 5), gains).astype(BF16).astype(F32)
        three_shifts(near.at[lev], wide)
    total = None
    for a in range(3):
        window = near[:, a * LAT : a * LAT + 128, :].reshape(512, 3 * D)
        part = dot(window, w_ref[layer, a])
        total = part if total is None else total + part
    finish(layer, total, x_refs, start, out_ref, 0, stage[0] if stage else None)
    if layer:
        copy = pltpu.make_async_copy(stage[0], out_ref.at[pl.ds(start * LAT, 128)], stage[1].at[0])
        copy.start()
        copy.wait()


def outer_kernel(layer, parts, lat_ref, *refs):
    x_refs, refs = refs[:parts], refs[parts:]
    west_ref, east_ref, w_ref, _ = refs[:4]
    refs = refs[4 + (1 if layer else 0) :]
    out_ref, near = refs[:2]
    stage = refs[2:]
    gain = gain_of(lat_ref[0], (LAT, D), 0)
    gains = jnp.concatenate([gain] * 5, axis=0)
    for lev in range(LEVELS):
        low = normal(read_x(x_refs, lev, 0, 5), gains).astype(BF16).astype(F32)
        three_shifts(near.at[lev, 0], jnp.concatenate([west_ref[lev].astype(F32), low], axis=0))
        high = normal(read_x(x_refs, lev, 11, 16), gains).astype(BF16).astype(F32)
        three_shifts(near.at[lev, 1], jnp.concatenate([high, east_ref[lev].astype(F32)], axis=0))
    for c in range(2):
        total = None
        for a in range(3):
            window = near[:, c, a * LAT : a * LAT + 128, :].reshape(512, 3 * D)
            part = dot(window, w_ref[layer, a])
            total = part if total is None else total + part
        finish(layer, total, x_refs, 12 * c, out_ref, 128 * c, stage[0] if stage else None)
    if layer:
        copies = [
            pltpu.make_async_copy(stage[0].at[pl.ds(0, 128)], out_ref.at[pl.ds(0, 128)], stage[1].at[0]),
            pltpu.make_async_copy(stage[0].at[pl.ds(128, 128)], out_ref.at[pl.ds(384, 128)], stage[1].at[1]),
        ]
        for copy in copies:
            copy.start()
        for copy in copies:
            copy.wait()


def rim_kernel(layer, parts, lat_ref, *refs):
    x_refs, refs = refs[:parts], refs[parts:]
    west_ref, east_ref, one_ref, two_ref, w_ref = refs[:5]
    refs = refs[5:]
    if layer:
        _, out_ref, taps, stage, stage_sems = refs
    else:
        outer_ref, rim_ref, west_out, east_out, one_out, two_out, taps = refs
    lat = lat_ref[0]
    odd = lax.rem(lat, 2) == 1
    gain = gain_of(lat, (LAT, D), 0)
    lon = iota((LON, D), 0)
    old = []
    for lev in range(LEVELS):
        row, col = iota((4 * LON, CELLS), 0), iota((4 * LON, CELLS), 1)
        lat_row = jnp.where(row < 2 * LON, row // LON, row // LON + LAT - 4)
        if parts == 1:
            pick = (col == row % LON * LAT + lat_row).astype(F32).astype(BF16)
            four = dot(pick, x_refs[0][lev])
        else:
            inner, inner_b, outer, rim = x_refs
            spot = (row % LON + 12) % LON
            spot = jnp.where(spot < 8, spot, jnp.where(spot >= 12, spot - 4, spot + 4))
            pick = (col == spot * LAT + lat_row).astype(F32).astype(BF16)
            four = dot(pick[:, :128], inner[lev]) + dot(pick[:, 128:256], inner_b[lev]) + dot(pick[:, 256:], outer[lev])
        rows = [four[n * LON : (n + 1) * LON] for n in range(4)]
        if parts > 1:
            rows[0] = rim[lev, 0:LON, :].astype(F32)
            rows[3] = rim[lev, LON:, :].astype(F32)
        old.append((rows[0], rows[3]))
        one, two = one_ref[lev].astype(F32), two_ref[lev].astype(F32)
        north = jnp.where(odd, one, two)
        south = jnp.where(odd, two, one)
        shifted = []
        for place, x in zip((0, 1, LAT - 2, LAT - 1), rows):
            u = normal(x, gain[place : place + 1, :]).astype(BF16).astype(F32)
            west = west_ref[lev, place : place + 1, :].astype(F32)
            east = east_ref[lev, place : place + 1, :].astype(F32)
            shifted.append((
                jnp.where(lon == 0, west, pltpu.roll(u, 1, axis=0)),
                u,
                jnp.where(lon == LON - 1, east, pltpu.roll(u, LON - 1, axis=0)),
            ))
        for a in range(3):
            top = jnp.concatenate([north[a : a + LON], shifted[0][a], shifted[1][a]], axis=1)
            low = jnp.concatenate([shifted[2][a], shifted[3][a], south[a : a + LON]], axis=1)
            taps[a, lev * 32 : lev * 32 + 16, :] = top.astype(BF16)
            taps[a, lev * 32 + 16 : lev * 32 + 32, :] = low.astype(BF16)
    total = None
    for a in range(3):
        part = dot(taps[a], w_ref[layer, a])
        total = part if total is None else total + part
    moved = gelu(total)
    copies = []
    for lev in range(LEVELS):
        top = (old[lev][0] + moved[lev * 32 : lev * 32 + 16]).astype(BF16)
        low = (old[lev][1] + moved[lev * 32 + 16 : lev * 32 + 32]).astype(BF16)
        if layer:
            stage[0:LON, lev, :] = top
            stage[LON:, lev, :] = low
            continue
        rim_ref[lev, 0:LON, :] = top
        rim_ref[lev, LON:, :] = low
        top, low = top.astype(F32), low.astype(F32)
        pair_rows(lat, lev, top, low, gain, one_out, two_out)
        place = iota((LAT, D), 0)
        for ref, start, k in ((west_out, 0, 0), (east_out, 7 * LAT, LON - 1)):
            column = outer_ref[lev, start : start + LAT, :].astype(F32)
            column = jnp.where(place == 0, top[k : k + 1], column)
            column = jnp.where(place == LAT - 1, low[k : k + 1], column)
            ref[lev] = normal(column, gain).astype(BF16)
    if layer:
        for k in range(LON):
            for side in range(2):
                copies.append(pltpu.make_async_copy(
                    stage.at[side * LON + k], out_ref.at[k * LAT + side * (LAT - 1)], stage_sems.at[side * LON + k]
                ))
        for copy in copies:
            copy.start()
        for copy in copies:
            copy.wait()


def corner_kernel(lat_ref, west_ref, east_ref, one_ref, two_ref, one_out, two_out):
    odd = lax.rem(lat_ref[0], 2) == 1
    for source, target, if_odd, if_even in ((one_ref, one_out, 0, LAT - 1), (two_ref, two_out, LAT - 1, 0)):
        for lev in range(LEVELS):
            ends = []
            for side in (west_ref, east_ref):
                rows = [side[lev, row : row + 1, :].astype(F32) for row in (if_odd, if_even)]
                ends.append(jnp.where(odd, rows[0], rows[1]))
            target[lev] = jnp.concatenate([ends[0], source[lev].astype(F32), ends[1]], axis=0).astype(BF16)


def pack_kernel(west_ref, east_ref, _, one_ref, two_ref):
    for slot, target in ((0, one_ref), (1, two_ref)):
        target[0] = west_ref[slot]
        target[1] = east_ref[slot]


def call(kernel, operands, outs, scratch, flops, name, alias=None):
    spaces = {"s": pltpu.SMEM, "v": pltpu.VMEM, "a": pl.ANY}
    out = pl.pallas_call(
        kernel,
        out_shape=tuple(shape for shape, _ in outs),
        in_specs=[pl.BlockSpec(memory_space=spaces[kind]) for _, kind in operands],
        out_specs=tuple(pl.BlockSpec(memory_space=spaces[kind]) for _, kind in outs),
        scratch_shapes=scratch,
        input_output_aliases=alias or {},
        compiler_params=pltpu.CompilerParams(vmem_limit_bytes=20 * MIB),
        cost_estimate=pl.CostEstimate(flops=flops, bytes_accessed=4 * MIB, transcendentals=0),
        name=name,
    )(*[array for array, _ in operands])
    return out[0] if len(out) == 1 else out


def layer_step(layer, lat, xs, west_u, east_u, one_u, two_u, weight):
    parts = len(xs)
    shape = jax.ShapeDtypeStruct
    state = [(lat, "s")] + [(x, "v") for x in xs]
    full = (shape((CELLS, LEVELS, D), BF16), "a")
    flops = 512 * 9 * D * D * 2

    def tile(rows):
        return (shape((LEVELS, rows, D), BF16), "v")

    def staging(cells, copies):
        return [pltpu.VMEM((cells, LEVELS, D), BF16), pltpu.SemaphoreType.DMA((copies,))] if layer else []

    def alias(operands):
        return {len(operands) - 1: 0} if layer else {}

    west = send(east_u, EAST)
    near = [pltpu.VMEM((LEVELS, 6 * LAT, 3 * D), BF16)]
    inner, west_u = call(
        functools.partial(inner_kernel, layer, parts, 0), state + [(weight, "v"), (west_u, "v")],
        [full if layer else tile(128), tile(LAT)], near + staging(128, 1), flops, "conv_inner",
    )
    east = send(west_u, WEST)
    operands = state + [(weight, "v")] + ([(inner, "a")] if layer else [])
    inner_b = call(
        functools.partial(inner_kernel, layer, parts, 1), operands,
        [full if layer else tile(128)], near + staging(128, 1), flops, "conv_inner", alias(operands),
    )
    one_u, two_u = call(
        corner_kernel, [(lat, "s"), (west, "v"), (east, "v"), (one_u, "v"), (two_u, "v")],
        [tile(LON + 2), tile(LON + 2)], [], 1000, "corners",
    )
    one = send(one_u, FIRST)
    two = send(two_u, SECOND)
    operands = state + [(west, "v"), (east, "v"), (weight, "v"), (one_u, "a")] + ([(inner_b, "a")] if layer else [])
    outer = call(
        functools.partial(outer_kernel, layer, parts), operands, [full if layer else tile(256)],
        [pltpu.VMEM((LEVELS, 2, 6 * LAT, 3 * D), BF16)] + staging(256, 2), 2 * flops, "conv_outer", alias(operands),
    )
    operands = state + [(west, "v"), (east, "v"), (one, "v"), (two, "v"), (weight, "v"), (outer, "a" if layer else "v")]
    done = call(
        functools.partial(rim_kernel, layer, parts), operands,
        [full] if layer else [tile(rows) for rows in (2 * LON, LAT, LAT, LON, LON)],
        [pltpu.VMEM((3, 128, 3 * D), BF16)] + staging(32, 32), flops // 4, "conv_rim", alias(operands),
    )
    return done if layer else ((inner, inner_b, outer, done[0]), *done[1:])


def route(target):
    pairs = []
    for lon in range(32):
        for lat in range(4):
            there = target(lon, lat)
            if there is not None:
                pairs.append((lon * 4 + lat, there[0] % 32 * 4 + there[1]))
    return pairs


EAST = route(lambda lon, lat: (lon + 1, lat))
WEST = route(lambda lon, lat: (lon - 1, lat))
FIRST = route(lambda lon, lat: (lon, lat ^ 1))
SECOND = route(lambda lon, lat: (lon + 16 if lat in (0, 3) else lon, (0, 2, 1, 3)[lat]))

MIDDLE = route(lambda lon, lat: (lon, 3 - lat) if lat in (1, 2) else None)


def send(block, pairs):
    return lax.ppermute(block, AXES, pairs)


def shards(
    patch_rows, source_embed, cell_embed, level_query, margin_rows, margin_counts,
    query_weight, key_weight, value_weight, out_weight, conv_weight,
):
    lat_place = lax.axis_index("lat")
    lat = lat_place.astype(jnp.int32).reshape(1)
    east_rows, west_rows, one_rows, two_rows, own = gather(lat, patch_rows, source_embed, margin_rows)
    from_west = send(east_rows, EAST)
    from_east = send(west_rows, WEST)
    one_own = send(one_rows, FIRST)
    two_own = send(two_rows, MIDDLE)

    def exchange(after):
        one, two = call(
            pack_kernel, [(from_west, "v"), (from_east, "v"), (after, "a")],
            [(jax.ShapeDtypeStruct((2, CAP, D), BF16), "v")] * 2, [], 1000, "pack",
        )
        return from_west, from_east, send(one, FIRST), send(two, MIDDLE)

    x, *sides = attention(lat, margin_counts.reshape(3, 1, 3), own, one_own, two_own, exchange,
                          cell_embed.reshape(CELLS, D), level_query, query_weight, key_weight, value_weight, out_weight)
    weight = conv_weight.reshape(2, 3, 3 * D, D)
    xs, *sides = layer_step(0, lat, (x,), *sides, weight)
    out = layer_step(1, lat, xs, *sides, weight)
    return out.reshape(LON, LAT, LEVELS, D)


def solution(mesh):
    placed = (
        P(AXES, None), P(), P("lon", "lat", None), P(), P(AXES, None, None, None), P(AXES, None, None),
        P(), P(), P(), P(), P(),
    )
    return jax.shard_map(
        shards, mesh=mesh, in_specs=placed, out_specs=P("lon", "lat", None, None), check_vma=False
    )
```

profile of v0, /device:TPU:1, one launch (start us, length us, event | category | flops | bytes accessed | tf_op | source)
XLA Modules:
  0.0 274.2 jit_solution(6237391500040726058)
XLA Ops:
  0.0 0.0 copy-start.1
  0.0 0.0 copy-start
  0.0 0.0 copy-start.8
  0.0 0.0 copy-start.2
  0.0 0.0 copy-start.3
  0.0 5.5 %gather_rows.1 = (bf16[3,128,512]{2,1,0:T(8,128)(2,1)}, bf16[3,128,512]{2,1,0:T(8,128)(2,1)}, bf16[128,512]{1,0:T(8,128)(2,1)}, bf16[128,512]{1,0:T(8,128)(2,1)}, bf16[128,512]{1,0:T(8,128)(2,1)}) custom-call(s32[1]{0:T(128)} %bitcast.lat_ref, bf16[2048,512]{1,0:T(8,128)(2,1)} %rows_hbm.1, bf16[4,512]{1,0:T(4,128)(2,1)} %embed_hbm.1, s32[9,1,128]{2,1,0:T(1,128)} %bitcast.21), custom_call_target="tpu_custom_call" | custom-call | tf_op jit(solution)/shard_map/gather_rows/pallas_call | solution.py:90
  5.5 1.5 collective-permute-start
  7.0 3.5 %collective-permute-start.1 = (bf16[128,512]{1,0:T(8,128)(2,1)}, bf16[128,512]{1,0:T(8,128)(2,1)S(1)}, u32[]{:S(2)}, u32[]{:S(2)}) collective-permute-start(bf16[128,512]{1,0:T(8,128)(2,1)} %get-tuple-element.38), channel_id=1, source_target_pairs={{1,2},{2,1},{5,6},{6,5},{9,10},{10,9},{13,14},{14,13},{17,18},{18,... | collective-permute-start | bytes 393224 | tf_op jit(solution)/shard_map/ppermute | solution.py:651
  10.6 1.4 collective-permute-start.2
  11.9 6.7 %collective-permute-start.3 = (bf16[3,128,512]{2,1,0:T(8,128)(2,1)}, bf16[3,128,512]{2,1,0:T(8,128)(2,1)S(1)}, u32[]{:S(2)}, u32[]{:S(2)}) collective-permute-start(bf16[3,128,512]{2,1,0:T(8,128)(2,1)} %get-tuple-element.40), channel_id=1, source_target_pairs={{0,124},{1,125},{2,126},{3,127},{4,0},{5,1},{6,2},{7,3},{8,4},{9,5... | collective-permute-start | bytes 1179656 | tf_op jit(solution)/shard_map/ppermute | solution.py:651
  18.7 0.0 collective-permute-done.one.one_own
  18.7 0.0 collective-permute-done.1.two.two_own
  18.7 0.0 copy-done.1
  18.7 0.0 copy-done
  18.7 0.0 copy-done.4
  18.7 0.0 copy-done.8
  18.7 0.0 copy-done.2
  18.7 0.0 copy-done.3
  18.7 0.0 copy-start.6
  18.7 0.9 copy-done.6
  19.6 7.2 %attend_first.1 = (f32[4,4,512,256]{3,2,1,0:T(8,128)S(1)}, bf16[512,512]{1,0:T(8,128)(2,1)S(1)}, bf16[4,128,512]{2,1,0:T(8,128)(2,1)S(1)}, f32[8,128]{1,0:T(8,128)S(1)}) custom-call(s32[1]{0:T(128)} %bitcast.lat_ref, s32[3,1,3]{2,1,0:T(1,128)S(1)} %bitcast.16, bf16[128,512]{1,0:T(8,128)(2,1)S(1)} %copy-done.6, ...), custom_call_target="tpu_custom_call" | custom-call | flops 3221225472 | bytes 4194304 | tf_op jit(solution)/shard_map/attend_first/pallas_call | solution.py:570
  26.8 0.0 collective-permute-done.2.west_ref.west
  26.8 0.0 collective-permute-done.3.east_ref.east
  26.9 0.1 collective-permute-start.4
  27.0 2.1 collective-permute-start.5
  29.1 0.0 copy-start.5
  29.1 0.0 copy-start.7
  29.1 0.0 slice-start
  29.1 0.0 slice-start.1
  29.1 5.2 %attend_second.1 = (f32[4,4,512,256]{3,2,1,0:T(8,128)S(1)}, f32[8,128]{1,0:T(8,128)S(1)}) custom-call(s32[1]{0:T(128)} %bitcast.lat_ref, s32[3,1,3]{2,1,0:T(1,128)S(1)} %bitcast.17, bf16[3,128,512]{2,1,0:T(8,128)(2,1)S(1)} %collective-permute-done.2.west_ref.west, ...), custom_call_target="tpu_custom_call", output_to_operand_aliasing={{0}: (4, {})} | custom-call | flops 2147483648 | bytes 4194304 | tf_op jit(solution)/shard_map/attend_second/pallas_call | solution.py:570
  34.3 0.0 collective-permute-done.4.one
  34.3 0.3 collective-permute-done.5.two
  34.7 0.0 copy-done.5
  34.7 0.0 copy-done.7
  34.7 186.2 %attend_third.1 = (bf16[4,512,512]{2,1,0:T(8,128)(2,1)S(1)}, bf16[4,32,512]{2,1,0:T(8,128)(2,1)S(1)}, bf16[4,32,512]{2,1,0:T(8,128)(2,1)S(1)}, bf16[4,16,512]{2,1,0:T(8,128)(2,1)S(1)}, bf16[4,16,512]{2,1,0:T(8,128)(2,1)S(1)}) custom-call(s32[1]{0:T(128)} %bitcast.lat_ref, s32[3,1,3]{2,1,0:T(1,128)S(1)} %bitcast.18, bf16[128,512]{1,0:T(8,128)(2,1)S(1)} %copy-done.7, ...), custom_call_target="tpu_custom_call" | custom-call | flops 4294967296 | bytes 4194304 | tf_op jit(solution)/shard_map/attend_third/pallas_call | solution.py:570
  220.8 0.3 collective-permute-start.6
  221.1 0.0 slice-done
  221.1 0.0 slice-done.1
  221.1 0.0 slice-done.2
  221.1 3.1 %conv_inner.4 = (bf16[4,128,512]{2,1,0:T(8,128)(2,1)S(1)}, bf16[4,32,512]{2,1,0:T(8,128)(2,1)S(1)}) custom-call(s32[1]{0:T(128)} %bitcast.lat_ref, bf16[4,512,512]{2,1,0:T(8,128)(2,1)S(1)} %get-tuple-element.49.refs_0_, bf16[2,3,1536,512]{3,2,1,0:T(8,128)(2,1)S(1)} %bitcast.8, bf16[4,32,512]{2,1,0:T(8,128)(2,1)S(1)} %get-tuple-element.50.refs_2_), custom_call_target="tpu_custom_call" | custom-call | flops 2415919104 | bytes 4194304 | tf_op jit(solution)/shard_map/conv_inner/pallas_call | solution.py:570
  224.2 7.6 %collective-permute-start.7 = (bf16[4,32,512]{2,1,0:T(8,128)(2,1)S(1)}, bf16[4,32,512]{2,1,0:T(8,128)(2,1)S(1)}, u32[]{:S(2)}, u32[]{:S(2)}) collective-permute-start(bf16[4,32,512]{2,1,0:T(8,128)(2,1)S(1)} %get-tuple-element.53), channel_id=1, source_target_pairs={{0,124},{1,125},{2,126},{3,127},{4,0},{5,1},{6,2},{7,3},{8,4},{9,5... | collective-permute-start | bytes 393224 | tf_op jit(solution)/shard_map/ppermute | solution.py:651
  231.8 3.0 %conv_inner.5.refs_1_ = bf16[4,128,512]{2,1,0:T(8,128)(2,1)S(1)} custom-call(s32[1]{0:T(128)} %bitcast.lat_ref, bf16[4,512,512]{2,1,0:T(8,128)(2,1)S(1)} %get-tuple-element.49.refs_0_, bf16[2,3,1536,512]{3,2,1,0:T(8,128)(2,1)S(1)} %bitcast.9), custom_call_target="tpu_custom_call" | custom-call | flops 2415919104 | bytes 4194304 | tf_op jit(solution)/shard_map/conv_inner/pallas_call | solution.py:570
  234.9 0.0 collective-permute-done.6.west_ref.refs_1_
  234.9 0.0 collective-permute-done.7.east_ref.refs_2_
  234.9 0.1 corners.2
  235.0 1.5 collective-permute-start.9
  236.5 0.2 collective-permute-start.8
  236.7 5.7 %conv_outer.2.refs_6_.refs_2_ = bf16[4,256,512]{2,1,0:T(8,128)(2,1)S(1)} custom-call(s32[1]{0:T(128)} %bitcast.lat_ref, bf16[4,512,512]{2,1,0:T(8,128)(2,1)S(1)} %get-tuple-element.49.refs_0_, bf16[4,32,512]{2,1,0:T(8,128)(2,1)S(1)} %collective-permute-done.6.west_ref.refs_1_, bf16[4,32,512]{2,1,0:T(8,128)(2,1)S(1)} %collective-permute-done.7.east_ref.refs_2_, ...), custom_call_target="tpu_custom_call" | custom-call | flops 4831838208 | bytes 4194304 | tf_op jit(solution)/shard_map/conv_outer/pallas_call | solution.py:570
  242.5 0.0 collective-permute-done.9.refs_4_
  242.5 0.0 collective-permute-done.8.refs_3_
  242.5 1.6 conv_rim.2
  244.1 0.3 collective-permute-start.10
  244.4 4.2 %conv_inner.6 = (bf16[512,4,512]{2,1,0:T(4,128)(2,1)}, bf16[4,32,512]{2,1,0:T(8,128)(2,1)S(1)}) custom-call(s32[1]{0:T(128)} %bitcast.lat_ref, bf16[4,128,512]{2,1,0:T(8,128)(2,1)S(1)} %get-tuple-element.51.refs_0_, bf16[4,128,512]{2,1,0:T(8,128)(2,1)S(1)} %conv_inner.5.refs_1_, bf16[4,256,512]{2,1,0:T(8,128)(2,1)S(1)} %conv_outer.2.refs_6_.refs_2_, ...), custom_call_target="tpu_custom_call" | custom-call | flops 2415919104 | bytes 4194304 | tf_op jit(solution)/shard_map/conv_inner/pallas_call | solution.py:570
  248.7 7.8 %collective-permute-start.11 = (bf16[4,32,512]{2,1,0:T(8,128)(2,1)S(1)}, bf16[4,32,512]{2,1,0:T(8,128)(2,1)S(1)}, u32[]{:S(2)}, u32[]{:S(2)}) collective-permute-start(bf16[4,32,512]{2,1,0:T(8,128)(2,1)S(1)} %get-tuple-element.61), channel_id=1, source_target_pairs={{0,124},{1,125},{2,126},{3,127},{4,0},{5,1},{6,2},{7,3},{8,4},{9,5... | collective-permute-start | bytes 393224 | tf_op jit(solution)/shard_map/ppermute | solution.py:651
  256.5 4.2 %conv_inner.7.refs_8_ = bf16[512,4,512]{2,1,0:T(4,128)(2,1)} custom-call(s32[1]{0:T(128)} %bitcast.lat_ref, bf16[4,128,512]{2,1,0:T(8,128)(2,1)S(1)} %get-tuple-element.51.refs_0_, bf16[4,128,512]{2,1,0:T(8,128)(2,1)S(1)} %conv_inner.5.refs_1_, bf16[4,256,512]{2,1,0:T(8,128)(2,1)S(1)} %conv_outer.2.refs_6_.refs_2_, ...), custom_call_target="tpu_custom_call", output_to_operand_aliasing={{}: (6, {})} | custom-call | flops 2415919104 | bytes 4194304 | tf_op jit(solution)/shard_map/conv_inner/pallas_call | solution.py:570
  260.7 0.0 collective-permute-done.10.west_ref.refs_4_
  260.8 0.0 collective-permute-done.11.east_ref.refs_5_
  260.8 0.1 corners.3
  260.9 0.2 collective-permute-start.13
  261.0 3.0 %collective-permute-start.12 = (bf16[4,18,512]{2,1,0:T(8,128)(2,1)S(1)}, bf16[4,18,512]{2,1,0:T(8,128)(2,1)S(1)}, u32[]{:S(2)}, u32[]{:S(2)}) collective-permute-start(bf16[4,18,512]{2,1,0:T(8,128)(2,1)S(1)} %get-tuple-element.64.refs_7_), channel_id=1, source_target_pairs={{0,1},{1,0},{2,3},{3,2},{4,5},{5,4},{6,7},{7,6},{8,9},{9,8},{10,11... | collective-permute-start | bytes 221192 | tf_op jit(solution)/shard_map/ppermute | solution.py:651
  264.0 7.5 %conv_outer.3.refs_9_ = bf16[512,4,512]{2,1,0:T(4,128)(2,1)} custom-call(s32[1]{0:T(128)} %bitcast.lat_ref, bf16[4,128,512]{2,1,0:T(8,128)(2,1)S(1)} %get-tuple-element.51.refs_0_, bf16[4,128,512]{2,1,0:T(8,128)(2,1)S(1)} %conv_inner.5.refs_1_, bf16[4,256,512]{2,1,0:T(8,128)(2,1)S(1)} %conv_outer.2.refs_6_.refs_2_, ...), custom_call_target="tpu_custom_call", output_to_operand_aliasing={{}: (9, {})} | custom-call | flops 4831838208 | bytes 4194304 | tf_op jit(solution)/shard_map/conv_outer/pallas_call | solution.py:570
  271.5 0.0 collective-permute-done.13.refs_7_
  271.5 0.0 collective-permute-done.12.refs_6_
  271.5 2.5 conv_rim.3
  (4 shorter events, 0.0 us)
Async XLA Ops:
  0.0 18.7 %copy-start.1 = (bf16[512,512]{1,0:T(8,128)(2,1)S(1)}, bf16[512,512]{1,0:T(8,128)(2,1)}, u32[]{:S(2)}) copy-start(bf16[512,512]{1,0:T(8,128)(2,1)} %wv_ref.5) | copy-start | bytes 1572868
  0.0 18.7 %copy-start = (bf16[512,512]{1,0:T(8,128)(2,1)S(1)}, bf16[512,512]{1,0:T(8,128)(2,1)}, u32[]{:S(2)}) copy-start(bf16[512,512]{1,0:T(8,128)(2,1)} %wk_ref.5) | copy-start | bytes 1572868
  0.0 18.7 %copy-start.4 = (bf16[512,512]{1,0:T(8,128)(2,1)S(1)}, bf16[512,512]{1,0:T(8,128)(2,1)}, u32[]{:S(2)}) copy-start(bf16[512,512]{1,0:T(8,128)(2,1)} %wq_ref.3) | copy-start | bytes 1572868
  0.0 18.7 %copy-start.8 = (bf16[4,512]{1,0:T(4,128)(2,1)S(1)}, bf16[4,512]{1,0:T(4,128)(2,1)}, u32[]{:S(2)}) copy-start(bf16[4,512]{1,0:T(4,128)(2,1)} %level_ref.3) | copy-start | bytes 12292
  0.0 18.7 %copy-start.2 = (s32[1,3,3]{2,0,1:T(1,128)S(1)}, s32[1,3,3]{2,0,1:T(1,128)}, u32[]{:S(2)}) copy-start(s32[1,3,3]{2,0,1:T(1,128)} %param.16) | copy-start | bytes 112
  0.0 18.7 %copy-start.3 = (bf16[16,32,512]{2,1,0:T(8,128)(2,1)S(1)}, bf16[16,32,512]{2,1,0:T(8,128)(2,1)}, u32[]{:S(2)}) copy-start(bf16[16,32,512]{2,1,0:T(8,128)(2,1)} %param.13) | copy-start | bytes 1572868
  5.5 13.1 %collective-permute-start = (bf16[128,512]{1,0:T(8,128)(2,1)}, bf16[128,512]{1,0:T(8,128)(2,1)S(1)}, u32[]{:S(2)}, u32[]{:S(2)}) collective-permute-start(bf16[128,512]{1,0:T(8,128)(2,1)} %get-tuple-element.37), channel_id=1, source_target_pairs={{0,1},{1,0},{2,3},{3,2},{4,5},{5,4},{6,7},{7,6},{8,9},{9,8},{10,11... | collective-permute-start | bytes 393224 | tf_op jit(solution)/shard_map/ppermute | solution.py:651
  7.0 11.7 %collective-permute-start.1 = (bf16[128,512]{1,0:T(8,128)(2,1)}, bf16[128,512]{1,0:T(8,128)(2,1)S(1)}, u32[]{:S(2)}, u32[]{:S(2)}) collective-permute-start(bf16[128,512]{1,0:T(8,128)(2,1)} %get-tuple-element.38), channel_id=1, source_target_pairs={{1,2},{2,1},{5,6},{6,5},{9,10},{10,9},{13,14},{14,13},{17,18},{18,... | collective-permute-start | bytes 393224 | tf_op jit(solution)/shard_map/ppermute | solution.py:651
  10.6 16.2 %collective-permute-start.2 = (bf16[3,128,512]{2,1,0:T(8,128)(2,1)}, bf16[3,128,512]{2,1,0:T(8,128)(2,1)S(1)}, u32[]{:S(2)}, u32[]{:S(2)}) collective-permute-start(bf16[3,128,512]{2,1,0:T(8,128)(2,1)} %get-tuple-element.39), channel_id=1, source_target_pairs={{0,4},{1,5},{2,6},{3,7},{4,8},{5,9},{6,10},{7,11},{8,12},{9,13},{1... | collective-permute-start | bytes 1179656 | tf_op jit(solution)/shard_map/ppermute | solution.py:651
  11.9 14.9 %collective-permute-start.3 = (bf16[3,128,512]{2,1,0:T(8,128)(2,1)}, bf16[3,128,512]{2,1,0:T(8,128)(2,1)S(1)}, u32[]{:S(2)}, u32[]{:S(2)}) collective-permute-start(bf16[3,128,512]{2,1,0:T(8,128)(2,1)} %get-tuple-element.40), channel_id=1, source_target_pairs={{0,124},{1,125},{2,126},{3,127},{4,0},{5,1},{6,2},{7,3},{8,4},{9,5... | collective-permute-start | bytes 1179656 | tf_op jit(solution)/shard_map/ppermute | solution.py:651
  18.7 0.9 copy-start.6
  26.9 7.4 %collective-permute-start.4 = (bf16[2,128,512]{2,1,0:T(8,128)(2,1)S(1)}, bf16[2,128,512]{2,1,0:T(8,128)(2,1)S(1)}, u32[]{:S(2)}, u32[]{:S(2)}) collective-permute-start(bf16[2,128,512]{2,1,0:T(8,128)(2,1)S(1)} %get-tuple-element.42), channel_id=1, source_target_pairs={{0,1},{1,0},{2,3},{3,2},{4,5},{5,4},{6,7},{7,6},{8,9},{9,8},{10,11... | collective-permute-start | bytes 786440 | tf_op jit(solution)/shard_map/ppermute | solution.py:651
  27.0 7.7 %collective-permute-start.5 = (bf16[2,128,512]{2,1,0:T(8,128)(2,1)S(1)}, bf16[2,128,512]{2,1,0:T(8,128)(2,1)S(1)}, u32[]{:S(2)}, u32[]{:S(2)}) collective-permute-start(bf16[2,128,512]{2,1,0:T(8,128)(2,1)S(1)} %get-tuple-element.43), channel_id=1, source_target_pairs={{1,2},{2,1},{5,6},{6,5},{9,10},{10,9},{13,14},{14,13},{17,18},{18,... | collective-permute-start | bytes 786440 | tf_op jit(solution)/shard_map/ppermute | solution.py:651
  29.1 5.6 %copy-start.5 = (bf16[512,512]{1,0:T(8,128)(2,1)S(1)}, bf16[512,512]{1,0:T(8,128)(2,1)}, u32[]{:S(2)}) copy-start(bf16[512,512]{1,0:T(8,128)(2,1)} %wo_ref.1) | copy-start | bytes 1572868
  29.1 5.6 %copy-start.7 = (bf16[128,512]{1,0:T(8,128)(2,1)S(1)}, bf16[128,512]{1,0:T(8,128)(2,1)}, u32[]{:S(2)}) copy-start(bf16[128,512]{1,0:T(8,128)(2,1)} %get-tuple-element.36.own) | copy-start | bytes 393220
  29.1 192.0 %slice-start = ((s8[9437184]{0:T(1024)(128)(4,1)}), s8[4194304]{0:T(1024)(128)(4,1)S(1)}, s32[]{:S(2)}) async-start(s8[9437184]{0:T(1024)(128)(4,1)} %bitcast.6), calls=%async_computation | async-start | bytes 8388608
  29.1 192.0 %slice-start.1 = ((s8[9437184]{0:T(1024)(128)(4,1)}), s8[4194304]{0:T(1024)(128)(4,1)S(1)}, s32[]{:S(2)}) async-start(s8[9437184]{0:T(1024)(128)(4,1)} %bitcast.6), calls=%async_computation.1 | async-start | bytes 8388608
  34.7 186.5 %slice-start.2 = ((s8[9437184]{0:T(1024)(128)(4,1)}), s8[1048576]{0:T(1024)(128)(4,1)S(1)}, s32[]{:S(2)}) async-start(s8[9437184]{0:T(1024)(128)(4,1)} %bitcast.6), calls=%async_computation.2 | async-start | bytes 2097152
  220.8 14.0 %collective-permute-start.6 = (bf16[4,32,512]{2,1,0:T(8,128)(2,1)S(1)}, bf16[4,32,512]{2,1,0:T(8,128)(2,1)S(1)}, u32[]{:S(2)}, u32[]{:S(2)}) collective-permute-start(bf16[4,32,512]{2,1,0:T(8,128)(2,1)S(1)} %get-tuple-element.52), channel_id=1, source_target_pairs={{0,4},{1,5},{2,6},{3,7},{4,8},{5,9},{6,10},{7,11},{8,12},{9,13},{1... | collective-permute-start | bytes 393224 | tf_op jit(solution)/shard_map/ppermute | solution.py:651
  224.2 10.7 %collective-permute-start.7 = (bf16[4,32,512]{2,1,0:T(8,128)(2,1)S(1)}, bf16[4,32,512]{2,1,0:T(8,128)(2,1)S(1)}, u32[]{:S(2)}, u32[]{:S(2)}) collective-permute-start(bf16[4,32,512]{2,1,0:T(8,128)(2,1)S(1)} %get-tuple-element.53), channel_id=1, source_target_pairs={{0,124},{1,125},{2,126},{3,127},{4,0},{5,1},{6,2},{7,3},{8,4},{9,5... | collective-permute-start | bytes 393224 | tf_op jit(solution)/shard_map/ppermute | solution.py:651
  235.0 7.5 %collective-permute-start.9 = (bf16[4,18,512]{2,1,0:T(8,128)(2,1)S(1)}, bf16[4,18,512]{2,1,0:T(8,128)(2,1)S(1)}, u32[]{:S(2)}, u32[]{:S(2)}) collective-permute-start(bf16[4,18,512]{2,1,0:T(8,128)(2,1)S(1)} %get-tuple-element.57), channel_id=1, source_target_pairs={{0,64},{1,2},{2,1},{3,67},{4,68},{5,6},{6,5},{7,71},{8,72},{9,10},... | collective-permute-start | bytes 221192 | tf_op jit(solution)/shard_map/ppermute | solution.py:651
  236.5 6.0 %collective-permute-start.8 = (bf16[4,18,512]{2,1,0:T(8,128)(2,1)S(1)}, bf16[4,18,512]{2,1,0:T(8,128)(2,1)S(1)}, u32[]{:S(2)}, u32[]{:S(2)}) collective-permute-start(bf16[4,18,512]{2,1,0:T(8,128)(2,1)S(1)} %get-tuple-element.56.refs_4_), channel_id=1, source_target_pairs={{0,1},{1,0},{2,3},{3,2},{4,5},{5,4},{6,7},{7,6},{8,9},{9,8},{10,11... | collective-permute-start | bytes 221192 | tf_op jit(solution)/shard_map/ppermute | solution.py:651
  244.1 16.6 %collective-permute-start.10 = (bf16[4,32,512]{2,1,0:T(8,128)(2,1)S(1)}, bf16[4,32,512]{2,1,0:T(8,128)(2,1)S(1)}, u32[]{:S(2)}, u32[]{:S(2)}) collective-permute-start(bf16[4,32,512]{2,1,0:T(8,128)(2,1)S(1)} %get-tuple-element.59), channel_id=1, source_target_pairs={{0,4},{1,5},{2,6},{3,7},{4,8},{5,9},{6,10},{7,11},{8,12},{9,13},{1... | collective-permute-start | bytes 393224 | tf_op jit(solution)/shard_map/ppermute | solution.py:651
  248.7 12.1 %collective-permute-start.11 = (bf16[4,32,512]{2,1,0:T(8,128)(2,1)S(1)}, bf16[4,32,512]{2,1,0:T(8,128)(2,1)S(1)}, u32[]{:S(2)}, u32[]{:S(2)}) collective-permute-start(bf16[4,32,512]{2,1,0:T(8,128)(2,1)S(1)} %get-tuple-element.61), channel_id=1, source_target_pairs={{0,124},{1,125},{2,126},{3,127},{4,0},{5,1},{6,2},{7,3},{8,4},{9,5... | collective-permute-start | bytes 393224 | tf_op jit(solution)/shard_map/ppermute | solution.py:651
  260.9 10.6 %collective-permute-start.13 = (bf16[4,18,512]{2,1,0:T(8,128)(2,1)S(1)}, bf16[4,18,512]{2,1,0:T(8,128)(2,1)S(1)}, u32[]{:S(2)}, u32[]{:S(2)}) collective-permute-start(bf16[4,18,512]{2,1,0:T(8,128)(2,1)S(1)} %get-tuple-element.65), channel_id=1, source_target_pairs={{0,64},{1,2},{2,1},{3,67},{4,68},{5,6},{6,5},{7,71},{8,72},{9,10},... | collective-permute-start | bytes 221192 | tf_op jit(solution)/shard_map/ppermute | solution.py:651
  261.0 10.5 %collective-permute-start.12 = (bf16[4,18,512]{2,1,0:T(8,128)(2,1)S(1)}, bf16[4,18,512]{2,1,0:T(8,128)(2,1)S(1)}, u32[]{:S(2)}, u32[]{:S(2)}) collective-permute-start(bf16[4,18,512]{2,1,0:T(8,128)(2,1)S(1)} %get-tuple-element.64.refs_7_), channel_id=1, source_target_pairs={{0,1},{1,0},{2,3},{3,2},{4,5},{5,4},{6,7},{7,6},{8,9},{9,8},{10,11... | collective-permute-start | bytes 221192 | tf_op jit(solution)/shard_map/ppermute | solution.py:651
where the time goes:
time: 274 us
  Pallas kernels  236 us (86%)
  starting transfers between devices  36.1 us (13%)
    pallas_call x14, Pallas kernels, call(): pl.pallas_call(kernel, out_shape=tuple((shape for shape, _ in outs)), in_...  231 us
    ppermute x14, starting transfers between devices, send(): return lax.ppermute(block, AXES, pairs)  36.1 us
    pallas_call x1, Pallas kernels, gather(): pl.pallas_call(gather_kernel, out_shape=(three, three, single, single, si...  5.49 us
  transfers between devices with their start and end apart: 14, of which 1 were waited for; matrix products, arithmetic and copies ran while one was open for 0% of the time, Pallas kernels for 15%

commit v1 on v0

--- a/solution.py
+++ b/solution.py
@@ -376,12 +376,13 @@
     return rows.reshape((high - low) * LAT, D)
 
 
-def interleave(stage, start, levels):
+def interleave(stage, start, levels, after):
     row, col = iota((256, 256), 0), iota((256, 256), 1)
     order = (col == row % LEVELS * 64 + row // LEVELS).astype(F32).astype(BF16)
     for half in range(2):
         rows = jnp.concatenate([y[half * 64 : half * 64 + 64] for y in levels], axis=0)
         stage[start + half * 64 : start + half * 64 + 64] = dot(order, rows).astype(BF16).reshape(64, LEVELS, D)
+        after(start + half * 64)
 
 
 def three_shifts(near, wide):
@@ -392,7 +393,7 @@
     near[:, 2 * D :] = jnp.where(row == LAT - 1, 0.0, pltpu.roll(wide, count - 1, axis=0)).astype(BF16)
 
 
-def finish(layer, total, x_refs, start, out_ref, place, stage):
+def finish(layer, total, x_refs, start, out_ref, place, stage, after):
     moved = gelu(total)
     levels = []
     for lev in range(LEVELS):
@@ -400,7 +401,7 @@
         if not layer:
             out_ref[lev, place : place + 128, :] = levels[lev]
     if layer:
-        interleave(stage, place, levels)
+        interleave(stage, place, levels, after)
 
 
 def inner_kernel(layer, parts, half, lat_ref, *refs):
@@ -427,10 +428,16 @@
         window = near[:, a * LAT : a * LAT + 128, :].reshape(512, 3 * D)
         part = dot(window, w_ref[layer, a])
         total = part if total is None else total + part
-    finish(layer, total, x_refs, start, out_ref, 0, stage[0] if stage else None)
-    if layer:
-        copy = pltpu.make_async_copy(stage[0], out_ref.at[pl.ds(start * LAT, 128)], stage[1].at[0])
-        copy.start()
+    copies = []
+
+    def after(place):
+        copies.append(pltpu.make_async_copy(
+            stage[0].at[pl.ds(place, 64)], out_ref.at[pl.ds(start * LAT + place, 64)], stage[1].at[len(copies)]
+        ))
+        copies[-1].start()
+
+    finish(layer, total, x_refs, start, out_ref, 0, stage[0] if stage else None, after)
+    for copy in copies:
         copy.wait()
 
 
@@ -447,22 +454,24 @@
         three_shifts(near.at[lev, 0], jnp.concatenate([west_ref[lev].astype(F32), low], axis=0))
         high = normal(read_x(x_refs, lev, 11, 16), gains).astype(BF16).astype(F32)
         three_shifts(near.at[lev, 1], jnp.concatenate([high, east_ref[lev].astype(F32)], axis=0))
+    copies = []
+
+    def after(place):
+        target = place if place < 128 else place + 256
+        copies.append(pltpu.make_async_copy(
+            stage[0].at[pl.ds(place, 64)], out_ref.at[pl.ds(target, 64)], stage[1].at[len(copies)]
+        ))
+        copies[-1].start()
+
     for c in range(2):
         total = None
         for a in range(3):
             window = near[:, c, a * LAT : a * LAT + 128, :].reshape(512, 3 * D)
             part = dot(window, w_ref[layer, a])
             total = part if total is None else total + part
-        finish(layer, total, x_refs, 12 * c, out_ref, 128 * c, stage[0] if stage else None)
-    if layer:
-        copies = [
-            pltpu.make_async_copy(stage[0].at[pl.ds(0, 128)], out_ref.at[pl.ds(0, 128)], stage[1].at[0]),
-            pltpu.make_async_copy(stage[0].at[pl.ds(128, 128)], out_ref.at[pl.ds(384, 128)], stage[1].at[1]),
-        ]
-        for copy in copies:
-            copy.start()
-        for copy in copies:
-            copy.wait()
+        finish(layer, total, x_refs, 12 * c, out_ref, 128 * c, stage[0] if stage else None, after)
+    for copy in copies:
+        copy.wait()
 
 
 def rim_kernel(layer, parts, lat_ref, *refs):
@@ -601,13 +610,13 @@
     near = [pltpu.VMEM((LEVELS, 6 * LAT, 3 * D), BF16)]
     inner, west_u = call(
         functools.partial(inner_kernel, layer, parts, 0), state + [(weight, "v"), (west_u, "v")],
-        [full if layer else tile(128), tile(LAT)], near + staging(128, 1), flops, "conv_inner",
+        [full if layer else tile(128), tile(LAT)], near + staging(128, 2), flops, "conv_inner",
     )
     east = send(west_u, WEST)
     operands = state + [(weight, "v")] + ([(inner, "a")] if layer else [])
     inner_b = call(
         functools.partial(inner_kernel, layer, parts, 1), operands,
-        [full if layer else tile(128)], near + staging(128, 1), flops, "conv_inner", alias(operands),
+        [full if layer else tile(128)], near + staging(128, 2), flops, "conv_inner", alias(operands),
     )
     one_u, two_u = call(
         corner_kernel, [(lat, "s"), (west, "v"), (east, "v"), (one_u, "v"), (two_u, "v")],
@@ -618,7 +627,7 @@
     operands = state + [(west, "v"), (east, "v"), (weight, "v"), (one_u, "a")] + ([(inner_b, "a")] if layer else [])
     outer = call(
         functools.partial(outer_kernel, layer, parts), operands, [full if layer else tile(256)],
-        [pltpu.VMEM((LEVELS, 2, 6 * LAT, 3 * D), BF16)] + staging(256, 2), 2 * flops, "conv_outer", alias(operands),
+        [pltpu.VMEM((LEVELS, 2, 6 * LAT, 3 * D), BF16)] + staging(256, 4), 2 * flops, "conv_outer", alias(operands),
     )
     operands = state + [(west, "v"), (east, "v"), (one, "v"), (two, "v"), (weight, "v"), (outer, "a" if layer else "v")]
     done = call(

time: 274 us -> 274 us (level)
  no operation moved by 1% of the time
where the time goes in v1:
time: 274 us
  Pallas kernels  236 us (86%)
  starting transfers between devices  36.1 us (13%)
    pallas_call x14, Pallas kernels, call(): pl.pallas_call(kernel, out_shape=tuple((shape for shape, _ in outs)), in_...  230 us
    ppermute x14, starting transfers between devices, send(): return lax.ppermute(block, AXES, pairs)  36.1 us
    pallas_call x1, Pallas kernels, gather(): pl.pallas_call(gather_kernel, out_shape=(three, three, single, single, si...  5.49 us
  transfers between devices with their start and end apart: 14, of which 1 were waited for; matrix products, arithmetic and copies ran while one was open for 0% of the time, Pallas kernels for 15%

profile of v1, /device:TPU:1, one launch (start us, length us, event | category | flops | bytes accessed | tf_op | source)
XLA Modules:
  0.0 273.8 jit_solution(915687898532671159)
XLA Ops:
  0.0 0.0 copy-start.1
  0.0 0.0 copy-start
  0.0 0.0 copy-start.8
  0.0 0.0 copy-start.2
  0.0 0.0 copy-start.3
  0.0 5.5 %gather_rows.1 = (bf16[3,128,512]{2,1,0:T(8,128)(2,1)}, bf16[3,128,512]{2,1,0:T(8,128)(2,1)}, bf16[128,512]{1,0:T(8,128)(2,1)}, bf16[128,512]{1,0:T(8,128)(2,1)}, bf16[128,512]{1,0:T(8,128)(2,1)}) custom-call(s32[1]{0:T(128)} %bitcast.lat_ref, bf16[2048,512]{1,0:T(8,128)(2,1)} %rows_hbm.1, bf16[4,512]{1,0:T(4,128)(2,1)} %embed_hbm.1, s32[9,1,128]{2,1,0:T(1,128)} %bitcast.21), custom_call_target="tpu_custom_call" | custom-call | tf_op jit(solution)/shard_map/gather_rows/pallas_call | solution.py:90
  5.5 1.5 collective-permute-start
  7.0 3.5 %collective-permute-start.1 = (bf16[128,512]{1,0:T(8,128)(2,1)}, bf16[128,512]{1,0:T(8,128)(2,1)S(1)}, u32[]{:S(2)}, u32[]{:S(2)}) collective-permute-start(bf16[128,512]{1,0:T(8,128)(2,1)} %get-tuple-element.38), channel_id=1, source_target_pairs={{1,2},{2,1},{5,6},{6,5},{9,10},{10,9},{13,14},{14,13},{17,18},{18,... | collective-permute-start | bytes 393224 | tf_op jit(solution)/shard_map/ppermute | solution.py:660
  10.6 1.4 collective-permute-start.2
  11.9 6.7 %collective-permute-start.3 = (bf16[3,128,512]{2,1,0:T(8,128)(2,1)}, bf16[3,128,512]{2,1,0:T(8,128)(2,1)S(1)}, u32[]{:S(2)}, u32[]{:S(2)}) collective-permute-start(bf16[3,128,512]{2,1,0:T(8,128)(2,1)} %get-tuple-element.40), channel_id=1, source_target_pairs={{0,124},{1,125},{2,126},{3,127},{4,0},{5,1},{6,2},{7,3},{8,4},{9,5... | collective-permute-start | bytes 1179656 | tf_op jit(solution)/shard_map/ppermute | solution.py:660
  18.7 0.0 collective-permute-done.one.one_own
  18.7 0.0 collective-permute-done.1.two.two_own
  18.7 0.0 copy-done.1
  18.7 0.0 copy-done
  18.7 0.0 copy-done.4
  18.7 0.0 copy-done.8
  18.7 0.0 copy-done.2
  18.7 0.0 copy-done.3
  18.7 0.0 copy-start.6
  18.7 0.9 copy-done.6
  19.6 7.2 %attend_first.1 = (f32[4,4,512,256]{3,2,1,0:T(8,128)S(1)}, bf16[512,512]{1,0:T(8,128)(2,1)S(1)}, bf16[4,128,512]{2,1,0:T(8,128)(2,1)S(1)}, f32[8,128]{1,0:T(8,128)S(1)}) custom-call(s32[1]{0:T(128)} %bitcast.lat_ref, s32[3,1,3]{2,1,0:T(1,128)S(1)} %bitcast.16, bf16[128,512]{1,0:T(8,128)(2,1)S(1)} %copy-done.6, ...), custom_call_target="tpu_custom_call" | custom-call | flops 3221225472 | bytes 4194304 | tf_op jit(solution)/shard_map/attend_first/pallas_call | solution.py:579
  26.8 0.0 collective-permute-done.2.west_ref.west
  26.8 0.0 collective-permute-done.3.east_ref.east
  26.9 0.1 collective-permute-start.4
  27.0 2.1 collective-permute-start.5
  29.1 0.0 copy-start.5
  29.1 0.0 copy-start.7
  29.1 0.0 slice-start
  29.1 0.0 slice-start.1
  29.1 5.2 %attend_second.1 = (f32[4,4,512,256]{3,2,1,0:T(8,128)S(1)}, f32[8,128]{1,0:T(8,128)S(1)}) custom-call(s32[1]{0:T(128)} %bitcast.lat_ref, s32[3,1,3]{2,1,0:T(1,128)S(1)} %bitcast.17, bf16[3,128,512]{2,1,0:T(8,128)(2,1)S(1)} %collective-permute-done.2.west_ref.west, ...), custom_call_target="tpu_custom_call", output_to_operand_aliasing={{0}: (4, {})} | custom-call | flops 2147483648 | bytes 4194304 | tf_op jit(solution)/shard_map/attend_second/pallas_call | solution.py:579
  34.3 0.0 collective-permute-done.4.one
  34.3 0.3 collective-permute-done.5.two
  34.7 0.0 copy-done.5
  34.7 0.0 copy-done.7
  34.7 186.2 %attend_third.1 = (bf16[4,512,512]{2,1,0:T(8,128)(2,1)S(1)}, bf16[4,32,512]{2,1,0:T(8,128)(2,1)S(1)}, bf16[4,32,512]{2,1,0:T(8,128)(2,1)S(1)}, bf16[4,16,512]{2,1,0:T(8,128)(2,1)S(1)}, bf16[4,16,512]{2,1,0:T(8,128)(2,1)S(1)}) custom-call(s32[1]{0:T(128)} %bitcast.lat_ref, s32[3,1,3]{2,1,0:T(1,128)S(1)} %bitcast.18, bf16[128,512]{1,0:T(8,128)(2,1)S(1)} %copy-done.7, ...), custom_call_target="tpu_custom_call" | custom-call | flops 4294967296 | bytes 4194304 | tf_op jit(solution)/shard_map/attend_third/pallas_call | solution.py:579
  220.8 0.3 collective-permute-start.6
  221.1 0.0 slice-done
  221.1 0.0 slice-done.1
  221.1 0.0 slice-done.2
  221.1 3.1 %conv_inner.4 = (bf16[4,128,512]{2,1,0:T(8,128)(2,1)S(1)}, bf16[4,32,512]{2,1,0:T(8,128)(2,1)S(1)}) custom-call(s32[1]{0:T(128)} %bitcast.lat_ref, bf16[4,512,512]{2,1,0:T(8,128)(2,1)S(1)} %get-tuple-element.49.refs_0_, bf16[2,3,1536,512]{3,2,1,0:T(8,128)(2,1)S(1)} %bitcast.8, bf16[4,32,512]{2,1,0:T(8,128)(2,1)S(1)} %get-tuple-element.50.refs_2_), custom_call_target="tpu_custom_call" | custom-call | flops 2415919104 | bytes 4194304 | tf_op jit(solution)/shard_map/conv_inner/pallas_call | solution.py:579
  224.2 7.6 %collective-permute-start.7 = (bf16[4,32,512]{2,1,0:T(8,128)(2,1)S(1)}, bf16[4,32,512]{2,1,0:T(8,128)(2,1)S(1)}, u32[]{:S(2)}, u32[]{:S(2)}) collective-permute-start(bf16[4,32,512]{2,1,0:T(8,128)(2,1)S(1)} %get-tuple-element.53), channel_id=1, source_target_pairs={{0,124},{1,125},{2,126},{3,127},{4,0},{5,1},{6,2},{7,3},{8,4},{9,5... | collective-permute-start | bytes 393224 | tf_op jit(solution)/shard_map/ppermute | solution.py:660
  231.8 3.0 %conv_inner.5.refs_1_ = bf16[4,128,512]{2,1,0:T(8,128)(2,1)S(1)} custom-call(s32[1]{0:T(128)} %bitcast.lat_ref, bf16[4,512,512]{2,1,0:T(8,128)(2,1)S(1)} %get-tuple-element.49.refs_0_, bf16[2,3,1536,512]{3,2,1,0:T(8,128)(2,1)S(1)} %bitcast.9), custom_call_target="tpu_custom_call" | custom-call | flops 2415919104 | bytes 4194304 | tf_op jit(solution)/shard_map/conv_inner/pallas_call | solution.py:579
  234.9 0.0 collective-permute-done.6.west_ref.refs_1_
  234.9 0.0 collective-permute-done.7.east_ref.refs_2_
  234.9 0.1 corners.2
  235.0 1.5 collective-permute-start.9
  236.5 0.2 collective-permute-start.8
  236.7 5.7 %conv_outer.2.refs_6_.refs_2_ = bf16[4,256,512]{2,1,0:T(8,128)(2,1)S(1)} custom-call(s32[1]{0:T(128)} %bitcast.lat_ref, bf16[4,512,512]{2,1,0:T(8,128)(2,1)S(1)} %get-tuple-element.49.refs_0_, bf16[4,32,512]{2,1,0:T(8,128)(2,1)S(1)} %collective-permute-done.6.west_ref.refs_1_, bf16[4,32,512]{2,1,0:T(8,128)(2,1)S(1)} %collective-permute-done.7.east_ref.refs_2_, ...), custom_call_target="tpu_custom_call" | custom-call | flops 4831838208 | bytes 4194304 | tf_op jit(solution)/shard_map/conv_outer/pallas_call | solution.py:579
  242.5 0.0 collective-permute-done.9.refs_4_
  242.5 0.0 collective-permute-done.8.refs_3_
  242.5 1.6 conv_rim.2
  244.1 0.3 collective-permute-start.10
  244.4 4.2 %conv_inner.6 = (bf16[512,4,512]{2,1,0:T(4,128)(2,1)}, bf16[4,32,512]{2,1,0:T(8,128)(2,1)S(1)}) custom-call(s32[1]{0:T(128)} %bitcast.lat_ref, bf16[4,128,512]{2,1,0:T(8,128)(2,1)S(1)} %get-tuple-element.51.refs_0_, bf16[4,128,512]{2,1,0:T(8,128)(2,1)S(1)} %conv_inner.5.refs_1_, bf16[4,256,512]{2,1,0:T(8,128)(2,1)S(1)} %conv_outer.2.refs_6_.refs_2_, ...), custom_call_target="tpu_custom_call" | custom-call | flops 2415919104 | bytes 4194304 | tf_op jit(solution)/shard_map/conv_inner/pallas_call | solution.py:579
  248.6 7.8 %collective-permute-start.11 = (bf16[4,32,512]{2,1,0:T(8,128)(2,1)S(1)}, bf16[4,32,512]{2,1,0:T(8,128)(2,1)S(1)}, u32[]{:S(2)}, u32[]{:S(2)}) collective-permute-start(bf16[4,32,512]{2,1,0:T(8,128)(2,1)S(1)} %get-tuple-element.61), channel_id=1, source_target_pairs={{0,124},{1,125},{2,126},{3,127},{4,0},{5,1},{6,2},{7,3},{8,4},{9,5... | collective-permute-start | bytes 393224 | tf_op jit(solution)/shard_map/ppermute | solution.py:660
  256.4 4.2 %conv_inner.7.refs_8_ = bf16[512,4,512]{2,1,0:T(4,128)(2,1)} custom-call(s32[1]{0:T(128)} %bitcast.lat_ref, bf16[4,128,512]{2,1,0:T(8,128)(2,1)S(1)} %get-tuple-element.51.refs_0_, bf16[4,128,512]{2,1,0:T(8,128)(2,1)S(1)} %conv_inner.5.refs_1_, bf16[4,256,512]{2,1,0:T(8,128)(2,1)S(1)} %conv_outer.2.refs_6_.refs_2_, ...), custom_call_target="tpu_custom_call", output_to_operand_aliasing={{}: (6, {})} | custom-call | flops 2415919104 | bytes 4194304 | tf_op jit(solution)/shard_map/conv_inner/pallas_call | solution.py:579
  260.6 0.0 collective-permute-done.10.west_ref.refs_4_
  260.6 0.0 collective-permute-done.11.east_ref.refs_5_
  260.6 0.1 corners.3
  260.7 0.2 collective-permute-start.13
  260.9 3.0 %collective-permute-start.12 = (bf16[4,18,512]{2,1,0:T(8,128)(2,1)S(1)}, bf16[4,18,512]{2,1,0:T(8,128)(2,1)S(1)}, u32[]{:S(2)}, u32[]{:S(2)}) collective-permute-start(bf16[4,18,512]{2,1,0:T(8,128)(2,1)S(1)} %get-tuple-element.64.refs_7_), channel_id=1, source_target_pairs={{0,1},{1,0},{2,3},{3,2},{4,5},{5,4},{6,7},{7,6},{8,9},{9,8},{10,11... | collective-permute-start | bytes 221192 | tf_op jit(solution)/shard_map/ppermute | solution.py:660
  263.8 7.3 %conv_outer.3.refs_9_ = bf16[512,4,512]{2,1,0:T(4,128)(2,1)} custom-call(s32[1]{0:T(128)} %bitcast.lat_ref, bf16[4,128,512]{2,1,0:T(8,128)(2,1)S(1)} %get-tuple-element.51.refs_0_, bf16[4,128,512]{2,1,0:T(8,128)(2,1)S(1)} %conv_inner.5.refs_1_, bf16[4,256,512]{2,1,0:T(8,128)(2,1)S(1)} %conv_outer.2.refs_6_.refs_2_, ...), custom_call_target="tpu_custom_call", output_to_operand_aliasing={{}: (9, {})} | custom-call | flops 4831838208 | bytes 4194304 | tf_op jit(solution)/shard_map/conv_outer/pallas_call | solution.py:579
  271.1 0.0 collective-permute-done.13.refs_7_
  271.1 0.0 collective-permute-done.12.refs_6_
  271.1 2.5 conv_rim.3
  (4 shorter events, 0.0 us)
Async XLA Ops:
  0.0 18.7 %copy-start.1 = (bf16[512,512]{1,0:T(8,128)(2,1)S(1)}, bf16[512,512]{1,0:T(8,128)(2,1)}, u32[]{:S(2)}) copy-start(bf16[512,512]{1,0:T(8,128)(2,1)} %wv_ref.5) | copy-start | bytes 1572868
  0.0 18.7 %copy-start = (bf16[512,512]{1,0:T(8,128)(2,1)S(1)}, bf16[512,512]{1,0:T(8,128)(2,1)}, u32[]{:S(2)}) copy-start(bf16[512,512]{1,0:T(8,128)(2,1)} %wk_ref.5) | copy-start | bytes 1572868
  0.0 18.7 %copy-start.4 = (bf16[512,512]{1,0:T(8,128)(2,1)S(1)}, bf16[512,512]{1,0:T(8,128)(2,1)}, u32[]{:S(2)}) copy-start(bf16[512,512]{1,0:T(8,128)(2,1)} %wq_ref.3) | copy-start | bytes 1572868
  0.0 18.7 %copy-start.8 = (bf16[4,512]{1,0:T(4,128)(2,1)S(1)}, bf16[4,512]{1,0:T(4,128)(2,1)}, u32[]{:S(2)}) copy-start(bf16[4,512]{1,0:T(4,128)(2,1)} %level_ref.3) | copy-start | bytes 12292
  0.0 18.7 %copy-start.2 = (s32[1,3,3]{2,0,1:T(1,128)S(1)}, s32[1,3,3]{2,0,1:T(1,128)}, u32[]{:S(2)}) copy-start(s32[1,3,3]{2,0,1:T(1,128)} %param.16) | copy-start | bytes 112
  0.0 18.7 %copy-start.3 = (bf16[16,32,512]{2,1,0:T(8,128)(2,1)S(1)}, bf16[16,32,512]{2,1,0:T(8,128)(2,1)}, u32[]{:S(2)}) copy-start(bf16[16,32,512]{2,1,0:T(8,128)(2,1)} %param.13) | copy-start | bytes 1572868
  5.5 13.1 %collective-permute-start = (bf16[128,512]{1,0:T(8,128)(2,1)}, bf16[128,512]{1,0:T(8,128)(2,1)S(1)}, u32[]{:S(2)}, u32[]{:S(2)}) collective-permute-start(bf16[128,512]{1,0:T(8,128)(2,1)} %get-tuple-element.37), channel_id=1, source_target_pairs={{0,1},{1,0},{2,3},{3,2},{4,5},{5,4},{6,7},{7,6},{8,9},{9,8},{10,11... | collective-permute-start | bytes 393224 | tf_op jit(solution)/shard_map/ppermute | solution.py:660
  7.0 11.7 %collective-permute-start.1 = (bf16[128,512]{1,0:T(8,128)(2,1)}, bf16[128,512]{1,0:T(8,128)(2,1)S(1)}, u32[]{:S(2)}, u32[]{:S(2)}) collective-permute-start(bf16[128,512]{1,0:T(8,128)(2,1)} %get-tuple-element.38), channel_id=1, source_target_pairs={{1,2},{2,1},{5,6},{6,5},{9,10},{10,9},{13,14},{14,13},{17,18},{18,... | collective-permute-start | bytes 393224 | tf_op jit(solution)/shard_map/ppermute | solution.py:660
  10.6 16.2 %collective-permute-start.2 = (bf16[3,128,512]{2,1,0:T(8,128)(2,1)}, bf16[3,128,512]{2,1,0:T(8,128)(2,1)S(1)}, u32[]{:S(2)}, u32[]{:S(2)}) collective-permute-start(bf16[3,128,512]{2,1,0:T(8,128)(2,1)} %get-tuple-element.39), channel_id=1, source_target_pairs={{0,4},{1,5},{2,6},{3,7},{4,8},{5,9},{6,10},{7,11},{8,12},{9,13},{1... | collective-permute-start | bytes 1179656 | tf_op jit(solution)/shard_map/ppermute | solution.py:660
  11.9 14.9 %collective-permute-start.3 = (bf16[3,128,512]{2,1,0:T(8,128)(2,1)}, bf16[3,128,512]{2,1,0:T(8,128)(2,1)S(1)}, u32[]{:S(2)}, u32[]{:S(2)}) collective-permute-start(bf16[3,128,512]{2,1,0:T(8,128)(2,1)} %get-tuple-element.40), channel_id=1, source_target_pairs={{0,124},{1,125},{2,126},{3,127},{4,0},{5,1},{6,2},{7,3},{8,4},{9,5... | collective-permute-start | bytes 1179656 | tf_op jit(solution)/shard_map/ppermute | solution.py:660
  18.7 0.9 copy-start.6
  26.9 7.4 %collective-permute-start.4 = (bf16[2,128,512]{2,1,0:T(8,128)(2,1)S(1)}, bf16[2,128,512]{2,1,0:T(8,128)(2,1)S(1)}, u32[]{:S(2)}, u32[]{:S(2)}) collective-permute-start(bf16[2,128,512]{2,1,0:T(8,128)(2,1)S(1)} %get-tuple-element.42), channel_id=1, source_target_pairs={{0,1},{1,0},{2,3},{3,2},{4,5},{5,4},{6,7},{7,6},{8,9},{9,8},{10,11... | collective-permute-start | bytes 786440 | tf_op jit(solution)/shard_map/ppermute | solution.py:660
  27.0 7.7 %collective-permute-start.5 = (bf16[2,128,512]{2,1,0:T(8,128)(2,1)S(1)}, bf16[2,128,512]{2,1,0:T(8,128)(2,1)S(1)}, u32[]{:S(2)}, u32[]{:S(2)}) collective-permute-start(bf16[2,128,512]{2,1,0:T(8,128)(2,1)S(1)} %get-tuple-element.43), channel_id=1, source_target_pairs={{1,2},{2,1},{5,6},{6,5},{9,10},{10,9},{13,14},{14,13},{17,18},{18,... | collective-permute-start | bytes 786440 | tf_op jit(solution)/shard_map/ppermute | solution.py:660
  29.1 5.6 %copy-start.5 = (bf16[512,512]{1,0:T(8,128)(2,1)S(1)}, bf16[512,512]{1,0:T(8,128)(2,1)}, u32[]{:S(2)}) copy-start(bf16[512,512]{1,0:T(8,128)(2,1)} %wo_ref.1) | copy-start | bytes 1572868
  29.1 5.6 %copy-start.7 = (bf16[128,512]{1,0:T(8,128)(2,1)S(1)}, bf16[128,512]{1,0:T(8,128)(2,1)}, u32[]{:S(2)}) copy-start(bf16[128,512]{1,0:T(8,128)(2,1)} %get-tuple-element.36.own) | copy-start | bytes 393220
  29.1 192.0 %slice-start = ((s8[9437184]{0:T(1024)(128)(4,1)}), s8[4194304]{0:T(1024)(128)(4,1)S(1)}, s32[]{:S(2)}) async-start(s8[9437184]{0:T(1024)(128)(4,1)} %bitcast.6), calls=%async_computation | async-start | bytes 8388608
  29.1 192.0 %slice-start.1 = ((s8[9437184]{0:T(1024)(128)(4,1)}), s8[4194304]{0:T(1024)(128)(4,1)S(1)}, s32[]{:S(2)}) async-start(s8[9437184]{0:T(1024)(128)(4,1)} %bitcast.6), calls=%async_computation.1 | async-start | bytes 8388608
  34.7 186.5 %slice-start.2 = ((s8[9437184]{0:T(1024)(128)(4,1)}), s8[1048576]{0:T(1024)(128)(4,1)S(1)}, s32[]{:S(2)}) async-start(s8[9437184]{0:T(1024)(128)(4,1)} %bitcast.6), calls=%async_computation.2 | async-start | bytes 2097152
  220.8 14.0 %collective-permute-start.6 = (bf16[4,32,512]{2,1,0:T(8,128)(2,1)S(1)}, bf16[4,32,512]{2,1,0:T(8,128)(2,1)S(1)}, u32[]{:S(2)}, u32[]{:S(2)}) collective-permute-start(bf16[4,32,512]{2,1,0:T(8,128)(2,1)S(1)} %get-tuple-element.52), channel_id=1, source_target_pairs={{0,4},{1,5},{2,6},{3,7},{4,8},{5,9},{6,10},{7,11},{8,12},{9,13},{1... | collective-permute-start | bytes 393224 | tf_op jit(solution)/shard_map/ppermute | solution.py:660
  224.2 10.7 %collective-permute-start.7 = (bf16[4,32,512]{2,1,0:T(8,128)(2,1)S(1)}, bf16[4,32,512]{2,1,0:T(8,128)(2,1)S(1)}, u32[]{:S(2)}, u32[]{:S(2)}) collective-permute-start(bf16[4,32,512]{2,1,0:T(8,128)(2,1)S(1)} %get-tuple-element.53), channel_id=1, source_target_pairs={{0,124},{1,125},{2,126},{3,127},{4,0},{5,1},{6,2},{7,3},{8,4},{9,5... | collective-permute-start | bytes 393224 | tf_op jit(solution)/shard_map/ppermute | solution.py:660
  235.0 7.5 %collective-permute-start.9 = (bf16[4,18,512]{2,1,0:T(8,128)(2,1)S(1)}, bf16[4,18,512]{2,1,0:T(8,128)(2,1)S(1)}, u32[]{:S(2)}, u32[]{:S(2)}) collective-permute-start(bf16[4,18,512]{2,1,0:T(8,128)(2,1)S(1)} %get-tuple-element.57), channel_id=1, source_target_pairs={{0,64},{1,2},{2,1},{3,67},{4,68},{5,6},{6,5},{7,71},{8,72},{9,10},... | collective-permute-start | bytes 221192 | tf_op jit(solution)/shard_map/ppermute | solution.py:660
  236.5 6.0 %collective-permute-start.8 = (bf16[4,18,512]{2,1,0:T(8,128)(2,1)S(1)}, bf16[4,18,512]{2,1,0:T(8,128)(2,1)S(1)}, u32[]{:S(2)}, u32[]{:S(2)}) collective-permute-start(bf16[4,18,512]{2,1,0:T(8,128)(2,1)S(1)} %get-tuple-element.56.refs_4_), channel_id=1, source_target_pairs={{0,1},{1,0},{2,3},{3,2},{4,5},{5,4},{6,7},{7,6},{8,9},{9,8},{10,11... | collective-permute-start | bytes 221192 | tf_op jit(solution)/shard_map/ppermute | solution.py:660
  244.1 16.5 %collective-permute-start.10 = (bf16[4,32,512]{2,1,0:T(8,128)(2,1)S(1)}, bf16[4,32,512]{2,1,0:T(8,128)(2,1)S(1)}, u32[]{:S(2)}, u32[]{:S(2)}) collective-permute-start(bf16[4,32,512]{2,1,0:T(8,128)(2,1)S(1)} %get-tuple-element.59), channel_id=1, source_target_pairs={{0,4},{1,5},{2,6},{3,7},{4,8},{5,9},{6,10},{7,11},{8,12},{9,13},{1... | collective-permute-start | bytes 393224 | tf_op jit(solution)/shard_map/ppermute | solution.py:660
  248.6 12.0 %collective-permute-start.11 = (bf16[4,32,512]{2,1,0:T(8,128)(2,1)S(1)}, bf16[4,32,512]{2,1,0:T(8,128)(2,1)S(1)}, u32[]{:S(2)}, u32[]{:S(2)}) collective-permute-start(bf16[4,32,512]{2,1,0:T(8,128)(2,1)S(1)} %get-tuple-element.61), channel_id=1, source_target_pairs={{0,124},{1,125},{2,126},{3,127},{4,0},{5,1},{6,2},{7,3},{8,4},{9,5... | collective-permute-start | bytes 393224 | tf_op jit(solution)/shard_map/ppermute | solution.py:660
  260.7 10.4 %collective-permute-start.13 = (bf16[4,18,512]{2,1,0:T(8,128)(2,1)S(1)}, bf16[4,18,512]{2,1,0:T(8,128)(2,1)S(1)}, u32[]{:S(2)}, u32[]{:S(2)}) collective-permute-start(bf16[4,18,512]{2,1,0:T(8,128)(2,1)S(1)} %get-tuple-element.65), channel_id=1, source_target_pairs={{0,64},{1,2},{2,1},{3,67},{4,68},{5,6},{6,5},{7,71},{8,72},{9,10},... | collective-permute-start | bytes 221192 | tf_op jit(solution)/shard_map/ppermute | solution.py:660
  260.9 10.3 %collective-permute-start.12 = (bf16[4,18,512]{2,1,0:T(8,128)(2,1)S(1)}, bf16[4,18,512]{2,1,0:T(8,128)(2,1)S(1)}, u32[]{:S(2)}, u32[]{:S(2)}) collective-permute-start(bf16[4,18,512]{2,1,0:T(8,128)(2,1)S(1)} %get-tuple-element.64.refs_7_), channel_id=1, source_target_pairs={{0,1},{1,0},{2,3},{3,2},{4,5},{5,4},{6,7},{7,6},{8,9},{9,8},{10,11... | collective-permute-start | bytes 221192 | tf_op jit(solution)/shard_map/ppermute | solution.py:660
